TPU v7x, 32 devices: a whole 2x2x4 slice. The times are simulated.
32 devices in a mesh: groups: 2 (over y), dp: 16 (over z, x, core).
Axes of the slice: x: 2, y: 2, z: 4, core: 2. Of those that a mesh axis runs over, the one named last changes fastest.
Arguments:
- acts: bfloat16 [8192, 5120], P(('groups', 'dp')), parts along dimension 0, may hold values from -6 to 6
- cotan: bfloat16 [8192, 1024], P(('groups', 'dp')), parts along dimension 0, may hold values from -4 to 4
- frozen_key_weight: bfloat16 [5120, 1024], P('dp'), may hold values from -0.078125 to 0.078125
- adapter_down_slots: bfloat16 [64, 5120, 128], P(('groups', 'dp')), parts along dimension 0, may hold values from -0.078125 to 0.078125
- adapter_up_slots: bfloat16 [64, 128, 1024], P(('groups', 'dp')), parts along dimension 0, may hold values from -0.5 to 0.5
- token_row_jobs: int32 [8192, 1], P(('groups', 'dp')), parts along dimension 0, may hold values from 0 to 31; in each aligned block of 256 rows (0 to 255, 256 to 511, ...) at most 16 rows name the same one
- slot_owner_jobs: int32 [64], P('groups'), parts along dimension 0, may hold values from 0 to 31, each once
- loss_token_count: int32 [64], P('groups'), parts along dimension 0, may hold values from 128 to 1023
Outputs:
- grad_acts: bfloat16 [8192, 5120], P(('groups', 'dp')), parts along dimension 0
- grad_a: bfloat16 [64, 5120, 128], P(('groups', 'dp')), parts along dimension 0
- grad_b: bfloat16 [64, 128, 1024], P(('groups', 'dp')), parts along dimension 0
There are 2 independent parts, one for each index of `groups`. A program takes and returns all parts, laid end to end along the dimension named above; an argument that names none is the same for every part. Nothing has to cross between parts.
Inputs may be any that keep to these rules, and one draw needn't show every extreme that they name: `token_row_jobs`: among the rows of one device no job is named by more than 16 rows, a bound that some block reaches; every job is named by some row. `slot_owner_jobs`: each job appears once; slot s lies on index s // 2 of dp.
All inputs are finite; a program needn't handle non-finite values.
Results may differ from a plain program's by a relative error of at most 0.0059.
Values may be sent and summed in bfloat16 or wider, within the bound.
No kernel may reach another device: no remote copies, remote signals or barrier semaphores. Data moves between devices by JAX's collectives and lax.ppermute only.
A program may use at most 128 MiB of HBM per device.

v0:
```python
import functools

import jax
import jax.numpy as jnp
from jax import lax
from jax.experimental import pallas as pl
from jax.experimental.pallas import tpu as pltpu
from jax.sharding import PartitionSpec as P

DELTA_MULTIPLIER = 0.25
BF = jnp.bfloat16
F32 = jnp.float32
PLANES = 4
PIECES = 4
PARAMS = pltpu.CompilerParams(vmem_limit_bytes=48 * 1024 * 1024)


def far(shape, dtype=BF):
    return pltpu.HBM(shape, dtype)


def whole(shape):
    zeros = (0,) * len(shape)
    return pl.BlockSpec(shape, lambda i: zeros)


def dot(a, b, ca=1, cb=0):
    return lax.dot_general(a, b, (((ca,), (cb,)), ((), ())), preferred_element_type=F32)


HERE = pl.BlockSpec(memory_space=pl.ANY)


def note_body(ref, out):
    out[...] = ref[...]


def note_step(line, note):
    return line.call(
        note_body,
        [note],
        [whole(note.shape)],
        whole(note.shape),
        jax.ShapeDtypeStruct(note.shape, note.dtype),
    )


def route_body(count, rows_ref, *refs):
    ins, outs = refs[:count], refs[count:]
    held = ins[0][...] if count == 1 else jnp.concatenate([r[...] for r in ins], axis=0)
    moved = dot(rows_ref[...], held).astype(BF)
    at = 0
    for out in outs:
        out[...] = moved[at : at + out.shape[0]]
        at += out.shape[0]


class Line:
    def __init__(self):
        self.last = []

    def call(self, body, operands, in_specs, out_specs, out_shape, pieces=1, scratch=()):
        after = self.last
        first = len(operands)
        many = isinstance(out_shape, list)

        def kernel(*refs):
            mark = len(refs) - 1 - len(scratch)
            refs[mark][...] = jnp.zeros_like(refs[mark])
            body(*refs[:first], *refs[first + len(after) : mark], *refs[mark + 1 :])

        out = pl.pallas_call(
            kernel,
            grid=(pieces,),
            in_specs=in_specs + [HERE] * len(after),
            out_specs=(out_specs if many else [out_specs]) + [whole((8, 128))],
            out_shape=(out_shape if many else [out_shape])
            + [jax.ShapeDtypeStruct((8, 128), jnp.int32)],
            scratch_shapes=scratch,
            compiler_params=PARAMS,
        )(*operands, *after)
        self.last = [out[-1]]
        return out[:-1] if many else out[0]


def route_body(count, rows_ref, *refs):
    ins, outs = refs[:count], refs[count:]
    held = ins[0][...] if count == 1 else jnp.concatenate([r[...] for r in ins], axis=0)
    moved = dot(rows_ref[...], held).astype(BF)
    at = 0
    for out in outs:
        out[...] = moved[at : at + out.shape[0]]
        at += out.shape[0]


class Line:
    def __init__(self):
        self.last = []

    def call(self, body, operands, in_specs, out_specs, out_shape, pieces=1, scratch=()):
        after = self.last
        first = len(operands)
        many = isinstance(out_shape, list)

        def kernel(*refs):
            mark = len(refs) - 1 - len(scratch)
            refs[mark][...] = jnp.zeros_like(refs[mark])
            body(*refs[:first], *refs[first + len(after) : mark], *refs[mark + 1 :])

        out = pl.pallas_call(
            kernel,
            grid=(pieces,),
            in_specs=in_specs + [HERE] * len(after),
            out_specs=(out_specs if many else [out_specs]) + [whole((8, 128))],
            out_shape=(out_shape if many else [out_shape])
            + [jax.ShapeDtypeStruct((8, 128), jnp.int32)],
            scratch_shapes=scratch,
            compiler_params=PARAMS,
        )(*operands, *after)
        self.last = [out[-1]]
        return out[:-1] if many else out[0]


def hold_body(ref, out):
    pass


def hold(line, x):
    last = line.last
    out = line.call(hold_body, [x], [FAR], FAR, far(x.shape, x.dtype), 1, {0: 0})
    line.last = last
    return out


def route(line, rows, ins, outs):
    width = ins[0].shape[1]
    pieces = PIECES if width % (128 * PIECES) == 0 else 1
    step = width // pieces
    return line.call(
        functools.partial(route_body, len(ins)),
        [rows, *ins],
        [whole(rows.shape)]
        + [pl.BlockSpec((x.shape[0], step), lambda i: (0, i)) for x in ins],
        [pl.BlockSpec((n, step), lambda i: (0, i)) for n in outs],
        [far((n, width)) for n in outs],
        pieces,
    )


def job_rows(refs, job):
    return jnp.concatenate([ref[job] for ref in refs], axis=0)


def back_body(count, up_ref, *refs):
    out = refs[count]
    for job in range(up_ref.shape[0]):
        held = job_rows(refs[:count], job)
        out[job] = (DELTA_MULTIPLIER * dot(held, up_ref[job], 1, 1)).astype(BF)


def back_project(line, up, rows):
    local, rank = up.shape[0], up.shape[1]
    shape = (local, sum(x.shape[1] for x in rows), rank)
    return line.call(
        functools.partial(back_body, len(rows)),
        [up, *rows],
        [whole(up.shape)] + [whole(x.shape) for x in rows],
        whole(shape),
        jax.ShapeDtypeStruct(shape, BF),
    )


def term_body(back_ref, down_ref, *outs):
    for job in range(down_ref.shape[0]):
        term = dot(back_ref[job], down_ref[job], 1, 1).astype(BF)
        at = 0
        for out in outs:
            out[job] = term[at : at + out.shape[1]]
            at += out.shape[1]


def adapter_terms(line, back_low, down, outs):
    local, width, rank = down.shape
    step = width // PIECES
    return line.call(
        term_body,
        [back_low, down],
        [whole(back_low.shape), pl.BlockSpec((local, step, rank), lambda i: (0, i, 0))],
        [pl.BlockSpec((local, n, step), lambda i: (0, 0, i)) for n in outs],
        [far((local, n, width)) for n in outs],
        PIECES,
    )


def owner_body(count, back_ref, down_ref, *refs):
    ins, (low_ref, grad_ref) = refs[:count], refs[count:]

    @pl.when(pl.program_id(0) == 0)
    def _():
        low_ref[...] = jnp.zeros_like(low_ref)

    for job in range(down_ref.shape[0]):
        held = job_rows(ins, job)
        low_ref[job] += dot(held, down_ref[job])
        grad_ref[job] = dot(held, back_ref[job], 0, 0).astype(BF)


def owner_step(line, back_low, down, rows):
    local, width, rank = down.shape
    step = width // PIECES
    part = pl.BlockSpec((local, step, rank), lambda i: (0, i, 0))
    low_shape = (local, back_low.shape[1], rank)
    return line.call(
        functools.partial(owner_body, len(rows)),
        [back_low, down, *rows],
        [whole(back_low.shape), part]
        + [pl.BlockSpec((local, x.shape[1], step), lambda i: (0, 0, i)) for x in rows],
        [whole(low_shape), part],
        [jax.ShapeDtypeStruct(low_shape, F32), jax.ShapeDtypeStruct(down.shape, BF)],
        PIECES,
    )


def up_body(count, low_ref, *refs):
    out = refs[count]
    for job in range(low_ref.shape[0]):
        low = low_ref[job].astype(BF)
        held = job_rows(refs[:count], job)
        out[job] = (DELTA_MULTIPLIER * dot(low, held, 0, 0)).astype(BF)


def up_gradient(line, low, rows):
    shape = (low.shape[0], low.shape[2], rows[0].shape[2])
    return line.call(
        functools.partial(up_body, len(rows)),
        [low, *rows],
        [whole(low.shape)] + [whole(x.shape) for x in rows],
        whole(shape),
        jax.ShapeDtypeStruct(shape, BF),
    )


def base_body(count, mine_ref, other_ref, *refs):
    ins, outs = refs[:count], refs[count:]
    lower = lax.axis_index("groups") == 0
    mine, other = mine_ref[0], other_ref[0]
    weight = jnp.concatenate(
        [jnp.where(lower, mine, other), jnp.where(lower, other, mine)], axis=0
    )
    for x, out in zip(ins, outs):
        out[...] = dot(weight, x[...], 1, 1).astype(BF)


def base_step(line, weight, rows):
    planes, share, deep = weight[0].shape
    step, tokens = 2 * share, rows[0].shape[0]
    half = pl.BlockSpec((1, share, deep), lambda i: (i, 0, 0))
    return line.call(
        functools.partial(base_body, len(rows)),
        [*weight, *rows],
        [half, half] + [whole(x.shape) for x in rows],
        [pl.BlockSpec((step, tokens), lambda i: (i, 0)) for _ in rows],
        [far((planes * step, tokens)) for _ in rows],
        planes,
    )


def final_body(count, rows_ref, came_ref, *refs):
    bases, out, held = refs[:count], refs[count], refs[count + 1]
    size = bases[0].shape[0]
    place = lax.rem(lax.axis_index("dp"), count)
    for s, ref in enumerate(bases):
        held[pl.ds(pl.multiple_of((place ^ s) * size, 16), size)] = ref[...]
    tokens = held.shape[1]
    one = (
        lax.broadcasted_iota(jnp.int32, (tokens, tokens), 0)
        == lax.broadcasted_iota(jnp.int32, (tokens, tokens), 1)
    ).astype(F32)
    base = dot(one.astype(BF), held[...], 1, 1)
    out[...] = (base + dot(rows_ref[...], came_ref[...])).astype(BF)


def final_step(line, rows, came, bases):
    tokens = rows.shape[0]
    step = came.shape[1] // PLANES
    size = step // len(bases)
    return line.call(
        functools.partial(final_body, len(bases)),
        [rows, came, *bases],
        [whole(rows.shape), pl.BlockSpec((came.shape[0], step), lambda i: (0, i))]
        + [pl.BlockSpec((size, tokens), lambda i: (i, 0)) for _ in bases],
        pl.BlockSpec((tokens, step), lambda i: (0, i)),
        jax.ShapeDtypeStruct((tokens, step * PLANES), BF),
        PLANES,
        [pltpu.VMEM((step, tokens), BF)],
    )


def shards(
    acts,
    cotan,
    frozen_key_weight,
    adapter_down_slots,
    adapter_up_slots,
    token_row_jobs,
    slot_owner_jobs,
    loss_token_count,
):
    devices = lax.axis_size("dp")
    parts = lax.axis_size("groups")
    tok_rows = acts.shape[0]
    local = adapter_down_slots.shape[0]
    jobs_all = slot_owner_jobs.shape[0]
    depth = 2 * tok_rows // (local * devices)
    column = devices // PLANES
    ring = column <= 4 and parts == 2
    most = local * column * depth
    segment = PLANES * depth
    me = lax.axis_index("dp")
    plane, place = me // column, me % column

    first = Line()
    stripes = [[p * column + c for p in range(PLANES)] for c in range(column)]
    ids = token_row_jobs[:, 0]
    lengths = loss_token_count.astype(F32)
    weights = jnp.mean(lengths) / lengths
    numbers = jnp.arange(jobs_all, dtype=jnp.int32)
    row_weight = jnp.sum(jnp.where(ids[:, None] == numbers[None, :], weights[None, :], 0.0), axis=1)
    row_slot = jnp.sum(
        jnp.where(ids[:, None] == slot_owner_jobs[None, :], numbers[None, :], 0), axis=1
    )
    scaled = (row_weight[:, None] * cotan.astype(F32)).astype(BF)

    planes = jnp.arange(PLANES, dtype=jnp.int32)
    need = jnp.max(
        jnp.sum((row_slot[:, None] // (local * column) == planes[None, :]).astype(jnp.int32), axis=0)
    )
    note = jnp.concatenate([row_slot, jnp.full((128,), need, jnp.int32)])
    share = frozen_key_weight.shape[0] // parts
    deep = frozen_key_weight.shape[1]
    own_share = lax.dynamic_slice_in_dim(
        frozen_key_weight, lax.axis_index("groups") * share, share, 0
    )
    if ring:
        shares = [own_share] + [
            lax.ppermute(
                own_share,
                "dp",
                [(d, ((d // column) ^ s) * column + d % column) for d in range(devices)],
            )
            for s in range(1, PLANES)
        ]
        first.last = [own_share]
        note = note_step(first, note[None])[0]
        near_share, far_shares = shares[1:2], shares[2:]
        shares = jnp.stack(shares)
        turn = jnp.arange(PLANES, dtype=jnp.int32) ^ plane
        weight_z = shares[0][None]
        for s in range(1, PLANES):
            weight_z = jnp.where((turn == s)[:, None, None], shares[s][None], weight_z)
    note = jnp.broadcast_to(note[None, None], (parts * devices, 1, tok_rows + 128))
    first.last = [note]
    notes = lax.all_to_all(
        note,
        ("groups", "dp"),
        split_axis=0,
        concat_axis=0,
        tiled=True,
    )[:, 0]
    need_all = jnp.max(notes[:, tok_rows])
    mine = notes[:, :tok_rows].reshape(parts, PLANES, column, tok_rows)
    mine = lax.dynamic_index_in_dim(mine, lax.axis_index("groups"), 0, keepdims=False)
    mine = lax.dynamic_index_in_dim(mine, place, 1, keepdims=False)
    slots = mine
    goal = slots // (local * column)
    earlier = jnp.arange(tok_rows)[None, :] < jnp.arange(tok_rows)[:, None]
    order = jnp.sum(
        ((goal[:, :, None] == goal[:, None, :]) & earlier[None]).astype(jnp.int32), axis=2
    )
    rank = jnp.sum(
        ((slots[:, :, None] == slots[:, None, :]) & earlier[None]).astype(jnp.int32), axis=2
    )
    owner = (slots // local) % column
    if ring:
        owner = owner ^ place
    spot = (
        owner * (local * segment)
        + (slots % local) * segment
        + planes[:, None] * depth
        + rank
    )
    spot = jnp.where(goal == plane, spot, -1)
    own_goal = row_slot // (local * column)
    own_order = jnp.sum(
        ((own_goal[:, None] == own_goal[None, :]) & earlier).astype(jnp.int32), axis=1
    )

    def across(bufs):
        return [bufs[0]] + [
            lax.ppermute(
                bufs[s],
                "dp",
                [(d, ((d // column) ^ s) * column + d % column) for d in range(devices)],
            )
            for s in range(1, PLANES)
        ]

    blocks = [[p * column + c for c in range(column)] for p in range(PLANES)]

    def within(x):
        return lax.all_to_all(
            x, "dp", split_axis=0, concat_axis=0, tiled=True, axis_index_groups=blocks
        )

    blocks_out = [local * segment] * column if ring else [column * local * segment]
    owner_outs = [segment] * column if ring else [column * segment]

    def near(bufs):
        if not ring:
            return [within(bufs[0])]
        return [bufs[0]] + [
            lax.ppermute(bufs[s], "dp", [(d, d ^ s) for d in range(devices)])
            for s in range(1, column)
        ]

    def at_owner(bufs):
        width = bufs[0].shape[1]
        if ring:
            return [x.reshape(local, segment, width) for x in bufs]
        x = bufs[0].reshape(column, local, segment, width).transpose(1, 0, 2, 3)
        return [x.reshape(local, column * segment, width)]

    def from_owner(bufs):
        width = bufs[0].shape[2]
        if ring:
            return [x.reshape(local * segment, width) for x in bufs]
        x = bufs[0].reshape(local, column, segment, width).transpose(1, 0, 2, 3)
        return [x.reshape(column * local * segment, width)]

    def planes_swap(x):
        return lax.all_to_all(
            x, "dp", split_axis=0, concat_axis=0, tiled=True, axis_index_groups=stripes
        )

    def gather_all(x, axis, groups=None):
        return lax.all_gather(x, axis, axis=0, tiled=True, axis_index_groups=groups)

    def outward(size, side):
        lanes = jnp.arange(PLANES * size, dtype=jnp.int32)
        code = side * size + own_order
        return (lanes[:, None] == code[None, :]).astype(BF), (
            code[:, None] == lanes[None, :]
        ).astype(BF)

    def inward(size, turned=False):
        kth = jnp.arange(size, dtype=jnp.int32)
        target = jnp.sum(
            jnp.where(
                (order[:, None, :] == kth[None, :, None]) & (spot[:, None, :] >= 0),
                spot[:, None, :] + 1,
                0,
            ),
            axis=2,
        )
        if turned:
            there = (planes ^ plane)[:, None, None] == planes[None, :, None]
            target = jnp.sum(jnp.where(there, target[None], 0), axis=1)
        target = target.reshape(PLANES * size) - 1
        spots = jnp.arange(PLANES * most, dtype=jnp.int32)
        return (spots[:, None] == target[None, :]).astype(BF), (
            target[:, None] == spots[None, :]
        ).astype(BF)

    rows_out = outward(most, own_goal ^ plane)[0]
    if ring:
        lanes = jnp.arange(tok_rows, dtype=jnp.int32)
        same_rows = (lanes[:, None] == lanes[None, :]).astype(BF)
        first.last += near_share
        early = route(first, same_rows, [scaled], [tok_rows])[0]
        mates = [
            early,
            *(lax.ppermute(early, "dp", [(d, d ^ s) for d in range(devices)]) for s in range(1, 3)),
        ]
        first.last += mates[1:2]
        late = route(first, same_rows, [scaled], [tok_rows])[0]
        mates += [
            lax.ppermute(late, "dp", [(d, d ^ s) for d in range(devices)])
            for s in range(3, column)
        ]
        mates = mates[:column]
        first.last += far_shares
    scaled_z = across(route(first, rows_out, [scaled], [most] * PLANES))
    steps = [most * 11 // 16, most * 13 // 16, most]
    total = PLANES * steps[0]
    usual = route(first, outward(steps[0], own_goal)[0], [acts], [total])[0]
    scaled_sent = route(first, inward(most, True)[0], scaled_z, blocks_out)

    def run(size):
        line = Line()
        total = PLANES * size
        out_rows, back_rows = outward(size, own_goal)
        spread, gather = inward(size)
        if ring:
            weight = weight_z, lax.ppermute(weight_z, "groups", [(0, 1), (1, 0)])
        else:
            weight = gather_all(frozen_key_weight, "dp")
        leaving = usual if size == steps[0] else route(line, out_rows, [acts], [total])[0]
        acts_z = planes_swap(leaving)
        got_scaled = at_owner(near(scaled_sent))
        back_low = back_project(line, adapter_up_slots, got_scaled)
        terms = adapter_terms(line, back_low, adapter_down_slots, owner_outs)
        terms = near(from_owner(terms))
        if ring:
            bases = near(base_step(line, weight, mates))
        else:
            bases = [dot(weight, scaled, 1, 1).astype(BF)]
        got = route(line, spread, [acts_z], blocks_out)
        came = planes_swap(route(line, gather, terms, [total])[0])
        got = at_owner(near(got))
        low, grad_a = owner_step(line, back_low, adapter_down_slots, got)
        grad_b = up_gradient(line, low, got_scaled)
        result = final_step(line, back_rows, came, bases)
        return result, grad_a, grad_b

    which = sum((need_all > s).astype(jnp.int32) for s in steps[:-1])
    return lax.switch(which, [functools.partial(run, s) for s in steps])


def solution(mesh):
    return jax.shard_map(
        shards,
        mesh=mesh,
        in_specs=(
            P(("groups", "dp"), None),
            P(("groups", "dp"), None),
            P("dp", None),
            P(("groups", "dp"), None, None),
            P(("groups", "dp"), None, None),
            P(("groups", "dp"), None),
            P("groups"),
            P("groups"),
        ),
        out_specs=(
            P(("groups", "dp"), None),
            P(("groups", "dp"), None, None),
            P(("groups", "dp"), None, None),
        ),
        check_vma=False,
    )
```

profile of v0, /device:TPU:1, one launch (start us, length us, event | category | flops | bytes accessed | tf_op | source)
XLA Modules:
  0.0 274.0 jit_solution(3275917704920723120)
XLA Ops:
  4.0 2.3 collective-permute-start.41
  9.7 7.0 %all-to-all-start.6 = ((s32[32,1,384]{2,1,0:T(1,128)}), s32[32,1,384]{2,1,0:T(1,128)S(1)}, u32[]{:S(2)}, u32[]{:S(2)}) async-start(s32[32,1,384]{2,1,0:T(1,128)} %broadcast_in_dim.174.refs_2_), calls=%async_computation.6 | async-start | bytes 98304 | tf_op jit(solution)/shard_map/all_to_all | solution.py:363
  18.9 19.6 %all-to-all-done.6 = s32[32,1,384]{2,1,0:T(1,128)S(1)} async-done(((s32[32,1,384]{2,1,0:T(1,128)}), s32[32,1,384]{2,1,0:T(1,128)S(1)}, u32[]{:S(2)}, u32[]{:S(2)}) %all-to-all-start.6) | async-done | bytes 49184 | tf_op jit(solution)/shard_map/all_to_all | solution.py:363
  56.0 3.4 %shard_map.107 = (bf16[352,5120]{1,0:T(8,128)(2,1)}, s32[8,128]{1,0:T(8,128)S(1)}) custom-call(bf16[352,256]{1,0:T(8,128)(2,1)S(1)} %fusion.17.refs_0_, bf16[256,5120]{1,0:T(8,128)(2,1)S(1)} %copy-done.33, s32[8,128]{1,0:T(8,128)S(1)} %get-tuple-element.250.refs_2_), custom_call_target="tpu_custom_call" | custom-call | tf_op jit(solution)/shard_map/pallas_call | solution.py:110
  59.3 4.1 %collective-permute-done.43.refs_2_ = bf16[128,1024]{1,0:T(8,128)(2,1)S(1)} collective-permute-done((bf16[128,1024]{1,0:T(8,128)(2,1)}, bf16[128,1024]{1,0:T(8,128)(2,1)S(1)}, u32[]{:S(2)}, u32[]{:S(2)}) %collective-permute-start.43) | collective-permute-done | bytes 262176 | tf_op jit(solution)/shard_map/ppermute | solution.py:400
  63.5 6.9 %collective-permute-done.45.refs_4_ = bf16[128,1024]{1,0:T(8,128)(2,1)S(1)} collective-permute-done((bf16[128,1024]{1,0:T(8,128)(2,1)}, bf16[128,1024]{1,0:T(8,128)(2,1)S(1)}, u32[]{:S(2)}, u32[]{:S(2)}) %collective-permute-start.45) | collective-permute-done | bytes 262176 | tf_op jit(solution)/shard_map/ppermute | solution.py:400
  70.4 2.3 shard_map.108
  72.7 200.2 %conditional.1 = (bf16[256,5120]{1,0:T(8,128)(2,1)}, bf16[2,5120,128]{2,1,0:T(8,128)(2,1)}, bf16[2,128,1024]{2,1,0:T(8,128)(2,1)}) conditional(s32[]{:T(128)} %clamp.11, (s32[256]{0:T(256)S(1)}, s32[256]{0:T(256)S(1)}, s32[4,256]{1,0:T(4,128)S(1)}, s32[4,256]{1,0:T(4,128)S(1)}, bf16[128,1024]{1,0:T(8,128)(2,1)}, ...), branch_computations={%region_11.13_spmd, %region_13.15_spmd, %region_15.17_spmd} | conditional | flops 2099712 | bytes 122204280 | solution.py:526
  72.8 8.3 %all-to-all-start = ((bf16[4,88,5120]{2,1,0:T(8,128)(2,1)}), bf16[4,88,5120]{2,1,0:T(8,128)(2,1)}, u32[]{:S(2)}, u32[]{:S(2)}) async-start(bf16[4,88,5120]{2,1,0:T(8,128)(2,1)} %bitcast.109), calls=%async_computation | async-start | bytes 7208960 | tf_op jit(solution)/shard_map/cond/branch_0_fun/all_to_all | solution.py:441
  84.8 5.9 %collective-permute-done.1 = bf16[128,1024]{1,0:T(8,128)(2,1)S(1)} collective-permute-done((bf16[128,1024]{1,0:T(8,128)(2,1)S(1)}, bf16[128,1024]{1,0:T(8,128)(2,1)S(1)}, u32[]{:S(2)}, u32[]{:S(2)}) %collective-permute-start.1) | collective-permute-done | bytes 262176 | tf_op jit(solution)/shard_map/cond/branch_0_fun/ppermute | solution.py:422
  90.7 6.1 %collective-permute-done.2 = bf16[128,1024]{1,0:T(8,128)(2,1)S(1)} collective-permute-done((bf16[128,1024]{1,0:T(8,128)(2,1)}, bf16[128,1024]{1,0:T(8,128)(2,1)S(1)}, u32[]{:S(2)}, u32[]{:S(2)}) %collective-permute-start.2) | collective-permute-done | bytes 262176 | tf_op jit(solution)/shard_map/cond/branch_0_fun/ppermute | solution.py:422
  99.1 3.8 %branch_0_fun.9 = (bf16[2,64,5120]{2,1,0:T(8,128)(2,1)}, bf16[2,64,5120]{2,1,0:T(8,128)(2,1)}, bf16[2,64,5120]{2,1,0:T(8,128)(2,1)}, bf16[2,64,5120]{2,1,0:T(8,128)(2,1)}, s32[8,128]{1,0:T(8,128)S(1)}) custom-call(bf16[2,256,128]{2,1,0:T(8,128)(2,1)S(1)} %get-tuple-element.105.refs_0_, bf16[2,5120,128]{2,1,0:T(8,128)(2,1)S(1)} %copy-done.32, ...), custom_call_target="tpu_custom_call" | custom-call | tf_op jit(solution)/shard_map/cond/branch_0_fun/pallas_call | solution.py:110
  105.7 9.3 %collective-permute-done.6.refs_1_ = bf16[4,160,1024]{2,1,0:T(8,128)(2,1)} collective-permute-done((bf16[4,160,1024]{2,1,0:T(8,128)(2,1)}, bf16[4,160,1024]{2,1,0:T(8,128)(2,1)}, u32[]{:S(2)}, u32[]{:S(2)}) %collective-permute-start.6) | collective-permute-done | bytes 1310752 | tf_op jit(solution)/shard_map/cond/branch_0_fun/ppermute | solution.py:504
  115.0 6.4 %branch_0_fun.10 = (bf16[1280,256]{1,0:T(8,128)(2,1)}, bf16[1280,256]{1,0:T(8,128)(2,1)}, bf16[1280,256]{1,0:T(8,128)(2,1)}, bf16[1280,256]{1,0:T(8,128)(2,1)}, s32[8,128]{1,0:T(8,128)S(1)}) custom-call(bf16[4,160,1024]{2,1,0:T(8,128)(2,1)} %get-tuple-element.113.refs_0_, bf16[4,160,1024]{2,1,0:T(8,128)(2,1)} %collective-permute-done.6.refs_1_, ...), custom_call_target="tpu_custom_call" | custom-call | tf_op jit(solution)/shard_map/cond/branch_0_fun/pallas_call | solution.py:110
  121.4 41.7 %all-to-all-done = bf16[4,88,5120]{2,1,0:T(8,128)(2,1)} async-done(((bf16[4,88,5120]{2,1,0:T(8,128)(2,1)}), bf16[4,88,5120]{2,1,0:T(8,128)(2,1)}, u32[]{:S(2)}, u32[]{:S(2)}) %all-to-all-start) | async-done | bytes 3604512 | tf_op jit(solution)/shard_map/cond/branch_0_fun/all_to_all | solution.py:441
  163.1 6.5 %branch_0_fun.11 = (bf16[128,5120]{1,0:T(8,128)(2,1)}, bf16[128,5120]{1,0:T(8,128)(2,1)}, bf16[128,5120]{1,0:T(8,128)(2,1)}, bf16[128,5120]{1,0:T(8,128)(2,1)}, s32[8,128]{1,0:T(8,128)S(1)}) custom-call(bf16[512,352]{1,0:T(8,128)(2,1)S(1)} %fusion.refs_0_, bf16[352,5120]{1,0:T(8,128)(2,1)} %bitcast.9.refs_1_, s32[8,128]{1,0:T(8,128)S(1)} %get-tuple-element.119.refs_2_), custom_call_target="tpu_custom_call" | custom-call | tf_op jit(solution)/shard_map/cond/branch_0_fun/pallas_call | solution.py:110
  169.6 5.4 %branch_0_fun.12 = (bf16[352,5120]{1,0:T(8,128)(2,1)}, s32[8,128]{1,0:T(8,128)S(1)}) custom-call(bf16[352,512]{1,0:T(8,128)(2,1)S(1)} %fusion.1.refs_0_, bf16[128,5120]{1,0:T(8,128)(2,1)S(1)} %bitcast.80, bf16[128,5120]{1,0:T(8,128)(2,1)S(1)} %collective-permute-done.3.refs_2_, bf16[128,5120]{1,0:T(8,128)(2,1)S(1)} %collective-permute-done.4.refs_3_, ...), custom_call_target="tpu_custom_call" | custom-call | tf_op jit(solution)/shard_map/cond/branch_0_fun/pallas_call | solution.py:110
  175.0 4.9 %all-to-all-start.1 = ((bf16[4,88,5120]{2,1,0:T(8,128)(2,1)}), bf16[4,88,5120]{2,1,0:T(8,128)(2,1)}, u32[]{:S(2)}, u32[]{:S(2)}) async-start(bf16[4,88,5120]{2,1,0:T(8,128)(2,1)} %bitcast.110), calls=%async_computation.1 | async-start | bytes 7208960 | tf_op jit(solution)/shard_map/cond/branch_0_fun/all_to_all | solution.py:441
  184.4 26.7 %collective-permute-done.11 = bf16[128,5120]{1,0:T(8,128)(2,1)S(1)} collective-permute-done((bf16[128,5120]{1,0:T(8,128)(2,1)}, bf16[128,5120]{1,0:T(8,128)(2,1)S(1)}, u32[]{:S(2)}, u32[]{:S(2)}) %collective-permute-start.11) | collective-permute-done | bytes 1310752 | tf_op jit(solution)/shard_map/cond/branch_0_fun/ppermute | solution.py:422
  211.1 29.0 %collective-permute-done.12 = bf16[128,5120]{1,0:T(8,128)(2,1)S(1)} collective-permute-done((bf16[128,5120]{1,0:T(8,128)(2,1)}, bf16[128,5120]{1,0:T(8,128)(2,1)S(1)}, u32[]{:S(2)}, u32[]{:S(2)}) %collective-permute-start.12) | collective-permute-done | bytes 1310752 | tf_op jit(solution)/shard_map/cond/branch_0_fun/ppermute | solution.py:422
  241.0 6.1 %branch_0_fun.13 = (f32[2,256,128]{2,1,0:T(8,128)S(1)}, bf16[2,5120,128]{2,1,0:T(8,128)(2,1)}, s32[8,128]{1,0:T(8,128)S(1)}) custom-call(bf16[2,256,128]{2,1,0:T(8,128)(2,1)S(1)} %copy-done.30, bf16[2,5120,128]{2,1,0:T(8,128)(2,1)} %get-tuple-element.106.refs_1_, bf16[2,64,5120]{2,1,0:T(8,128)(2,1)S(1)} %bitcast.66, bf16[2,64,5120]{2,1,0:T(8,128)(2,1)S(1)} %bitcast.69, ...), custom_call_target="tpu_custom_call" | custom-call | tf_op jit(solution)/shard_map/cond/branch_0_fun/pallas_call | solution.py:110
  248.3 5.0 %collective-permute-done.8.refs_4_ = bf16[1280,256]{1,0:T(8,128)(2,1)S(1)} collective-permute-done((bf16[1280,256]{1,0:T(8,128)(2,1)}, bf16[1280,256]{1,0:T(8,128)(2,1)S(1)}, u32[]{:S(2)}, u32[]{:S(2)}) %collective-permute-start.8) | collective-permute-done | bytes 655392 | tf_op jit(solution)/shard_map/cond/branch_0_fun/ppermute | solution.py:422
  253.3 14.1 %collective-permute-done.9.refs_5_ = bf16[1280,256]{1,0:T(8,128)(2,1)S(1)} collective-permute-done((bf16[1280,256]{1,0:T(8,128)(2,1)}, bf16[1280,256]{1,0:T(8,128)(2,1)S(1)}, u32[]{:S(2)}, u32[]{:S(2)}) %collective-permute-start.9) | collective-permute-done | bytes 655392 | tf_op jit(solution)/shard_map/cond/branch_0_fun/ppermute | solution.py:422
  267.4 5.5 %branch_0_fun.15 = (bf16[256,5120]{1,0:T(8,128)(2,1)}, s32[8,128]{1,0:T(8,128)}) custom-call(bf16[256,352]{1,0:T(8,128)(2,1)S(1)} %fusion.2.refs_0_, bf16[352,5120]{1,0:T(8,128)(2,1)} %bitcast.11.refs_1_, bf16[1280,256]{1,0:T(8,128)(2,1)S(1)} %copy-done.28, bf16[1280,256]{1,0:T(8,128)(2,1)S(1)} %collective-permute-done.7.refs_3_, ...), custom_call_target="tpu_custom_call" | custom-call | tf_op jit(solution)/shard_map/cond/branch_0_fun/pallas_call | solution.py:110
  (135 shorter events, 40.6 us)
Async XLA Ops:
  1.8 37.6 %collective-permute-start.39 = (bf16[160,1024]{1,0:T(8,128)(2,1)S(1)}, bf16[160,1024]{1,0:T(8,128)(2,1)S(1)}, u32[]{:S(2)}, u32[]{:S(2)}) collective-permute-start(bf16[160,1024]{1,0:T(8,128)(2,1)S(1)} %constant_dynamic-slice_fusion.1.refs_1_), channel_id=1, source_target_pairs={{0,4},{1,5},{2,6},{3,7},{4,0},{5,1},{6,2},{7,3},{8,12},{9,13},{10,... | collective-permute-start | bytes 983048 | tf_op jit(solution)/shard_map/ppermute | solution.py:346
  4.0 44.1 %collective-permute-start.41 = (bf16[160,1024]{1,0:T(8,128)(2,1)S(1)}, bf16[160,1024]{1,0:T(8,128)(2,1)S(1)}, u32[]{:S(2)}, u32[]{:S(2)}) collective-permute-start(bf16[160,1024]{1,0:T(8,128)(2,1)S(1)} %constant_dynamic-slice_fusion.1.refs_1_), channel_id=1, source_target_pairs={{0,8},{1,9},{2,10},{3,11},{4,12},{5,13},{6,14},{7,15},{8,0},{9,1},... | collective-permute-start | bytes 983048 | tf_op jit(solution)/shard_map/ppermute | solution.py:346
  6.3 41.8 %collective-permute-start.42 = (bf16[160,1024]{1,0:T(8,128)(2,1)S(1)}, bf16[160,1024]{1,0:T(8,128)(2,1)S(1)}, u32[]{:S(2)}, u32[]{:S(2)}) collective-permute-start(bf16[160,1024]{1,0:T(8,128)(2,1)S(1)} %constant_dynamic-slice_fusion.1.refs_1_), channel_id=1, source_target_pairs={{0,12},{1,13},{2,14},{3,15},{4,8},{5,9},{6,10},{7,11},{8,4},{9,5},... | collective-permute-start | bytes 983048 | tf_op jit(solution)/shard_map/ppermute | solution.py:346
  9.7 28.7 %all-to-all-start.6 = ((s32[32,1,384]{2,1,0:T(1,128)}), s32[32,1,384]{2,1,0:T(1,128)S(1)}, u32[]{:S(2)}, u32[]{:S(2)}) async-start(s32[32,1,384]{2,1,0:T(1,128)} %broadcast_in_dim.174.refs_2_), calls=%async_computation.6 | async-start | bytes 98304 | tf_op jit(solution)/shard_map/all_to_all | solution.py:363
  44.1 28.7 %collective-permute-start.46 = (bf16[256,1024]{1,0:T(8,128)(2,1)}, bf16[256,1024]{1,0:T(8,128)(2,1)}, u32[]{:S(2)}, u32[]{:S(2)}) collective-permute-start(bf16[256,1024]{1,0:T(8,128)(2,1)} %get-tuple-element.244), channel_id=1, source_target_pairs={{0,2},{1,3},{2,0},{3,1},{4,6},{5,7},{6,4},{7,5},{8,10},{9,11},{10,... | collective-permute-start | bytes 1572872 | tf_op jit(solution)/shard_map/ppermute | solution.py:482
  46.6 26.2 %collective-permute-start.47 = (bf16[256,1024]{1,0:T(8,128)(2,1)}, bf16[256,1024]{1,0:T(8,128)(2,1)}, u32[]{:S(2)}, u32[]{:S(2)}) collective-permute-start(bf16[256,1024]{1,0:T(8,128)(2,1)} %get-tuple-element.257), channel_id=1, source_target_pairs={{0,3},{1,2},{2,1},{3,0},{4,7},{5,6},{6,5},{7,4},{8,11},{9,10},{10,... | collective-permute-start | bytes 1572872 | tf_op jit(solution)/shard_map/ppermute | solution.py:487
  50.2 13.3 %collective-permute-start.43 = (bf16[128,1024]{1,0:T(8,128)(2,1)}, bf16[128,1024]{1,0:T(8,128)(2,1)S(1)}, u32[]{:S(2)}, u32[]{:S(2)}) collective-permute-start(bf16[128,1024]{1,0:T(8,128)(2,1)} %get-tuple-element.247), channel_id=1, source_target_pairs={{0,4},{1,5},{2,6},{3,7},{4,0},{5,1},{6,2},{7,3},{8,12},{9,13},{10,... | collective-permute-start | bytes 786440 | tf_op jit(solution)/shard_map/ppermute | solution.py:400
  50.5 13.0 %collective-permute-start.44 = (bf16[128,1024]{1,0:T(8,128)(2,1)}, bf16[128,1024]{1,0:T(8,128)(2,1)S(1)}, u32[]{:S(2)}, u32[]{:S(2)}) collective-permute-start(bf16[128,1024]{1,0:T(8,128)(2,1)} %get-tuple-element.248), channel_id=1, source_target_pairs={{0,8},{1,9},{2,10},{3,11},{4,12},{5,13},{6,14},{7,15},{8,0},{9,1},... | collective-permute-start | bytes 786440 | tf_op jit(solution)/shard_map/ppermute | solution.py:400
  52.7 17.7 %collective-permute-start.45 = (bf16[128,1024]{1,0:T(8,128)(2,1)}, bf16[128,1024]{1,0:T(8,128)(2,1)S(1)}, u32[]{:S(2)}, u32[]{:S(2)}) collective-permute-start(bf16[128,1024]{1,0:T(8,128)(2,1)} %get-tuple-element.249), channel_id=1, source_target_pairs={{0,12},{1,13},{2,14},{3,15},{4,8},{5,9},{6,10},{7,11},{8,4},{9,5},... | collective-permute-start | bytes 786440 | tf_op jit(solution)/shard_map/ppermute | solution.py:400
  72.8 90.3 %all-to-all-start = ((bf16[4,88,5120]{2,1,0:T(8,128)(2,1)}), bf16[4,88,5120]{2,1,0:T(8,128)(2,1)}, u32[]{:S(2)}, u32[]{:S(2)}) async-start(bf16[4,88,5120]{2,1,0:T(8,128)(2,1)} %bitcast.109), calls=%async_computation | async-start | bytes 7208960 | tf_op jit(solution)/shard_map/cond/branch_0_fun/all_to_all | solution.py:441
  81.1 3.7 %collective-permute-start = (bf16[128,1024]{1,0:T(8,128)(2,1)S(1)}, bf16[128,1024]{1,0:T(8,128)(2,1)S(1)}, u32[]{:S(2)}, u32[]{:S(2)}) collective-permute-start(bf16[128,1024]{1,0:T(8,128)(2,1)S(1)} %copy-done.47), channel_id=1, source_target_pairs={{0,1},{1,0},{2,3},{3,2},{4,5},{5,4},{6,7},{7,6},{8,9},{9,8},{10,11... | collective-permute-start | bytes 786440 | tf_op jit(solution)/shard_map/cond/branch_0_fun/ppermute | solution.py:422
  82.8 8.0 %collective-permute-start.1 = (bf16[128,1024]{1,0:T(8,128)(2,1)S(1)}, bf16[128,1024]{1,0:T(8,128)(2,1)S(1)}, u32[]{:S(2)}, u32[]{:S(2)}) collective-permute-start(bf16[128,1024]{1,0:T(8,128)(2,1)S(1)} %copy-done.50), channel_id=1, source_target_pairs={{0,2},{1,3},{2,0},{3,1},{4,6},{5,7},{6,4},{7,5},{8,10},{9,11},{10,... | collective-permute-start | bytes 786440 | tf_op jit(solution)/shard_map/cond/branch_0_fun/ppermute | solution.py:422
  83.2 13.7 %collective-permute-start.2 = (bf16[128,1024]{1,0:T(8,128)(2,1)}, bf16[128,1024]{1,0:T(8,128)(2,1)S(1)}, u32[]{:S(2)}, u32[]{:S(2)}) collective-permute-start(bf16[128,1024]{1,0:T(8,128)(2,1)} %get-tuple-element.104), channel_id=1, source_target_pairs={{0,3},{1,2},{2,1},{3,0},{4,7},{5,6},{6,5},{7,4},{8,11},{9,10},{10,... | collective-permute-start | bytes 786440 | tf_op jit(solution)/shard_map/cond/branch_0_fun/ppermute | solution.py:422
  84.5 30.5 %collective-permute-start.6 = (bf16[4,160,1024]{2,1,0:T(8,128)(2,1)}, bf16[4,160,1024]{2,1,0:T(8,128)(2,1)}, u32[]{:S(2)}, u32[]{:S(2)}) collective-permute-start(bf16[4,160,1024]{2,1,0:T(8,128)(2,1)} %get-tuple-element.113.refs_0_), channel_id=1, source_target_pairs={{0,16},{16,0},{1,17},{17,1},{2,18},{18,2},{3,19},{19,3},{4,20},{20... | collective-permute-start | bytes 3932168 | tf_op jit(solution)/shard_map/cond/branch_0_fun/ppermute | solution.py:504
  103.0 66.6 %collective-permute-start.3 = (bf16[128,5120]{1,0:T(8,128)(2,1)}, bf16[128,5120]{1,0:T(8,128)(2,1)S(1)}, u32[]{:S(2)}, u32[]{:S(2)}) collective-permute-start(bf16[128,5120]{1,0:T(8,128)(2,1)} %bitcast.123), channel_id=1, source_target_pairs={{0,1},{1,0},{2,3},{3,2},{4,5},{5,4},{6,7},{7,6},{8,9},{9,8},{10,11... | collective-permute-start | bytes 3932168 | tf_op jit(solution)/shard_map/cond/branch_0_fun/ppermute | solution.py:422
  103.0 66.6 %collective-permute-start.4 = (bf16[128,5120]{1,0:T(8,128)(2,1)}, bf16[128,5120]{1,0:T(8,128)(2,1)S(1)}, u32[]{:S(2)}, u32[]{:S(2)}) collective-permute-start(bf16[128,5120]{1,0:T(8,128)(2,1)} %bitcast.120), channel_id=1, source_target_pairs={{0,2},{1,3},{2,0},{3,1},{4,6},{5,7},{6,4},{7,5},{8,10},{9,11},{10,... | collective-permute-start | bytes 3932168 | tf_op jit(solution)/shard_map/cond/branch_0_fun/ppermute | solution.py:422
  103.5 66.1 %collective-permute-start.5 = (bf16[128,5120]{1,0:T(8,128)(2,1)}, bf16[128,5120]{1,0:T(8,128)(2,1)}, u32[]{:S(2)}, u32[]{:S(2)}) collective-permute-start(bf16[128,5120]{1,0:T(8,128)(2,1)} %bitcast.117), channel_id=1, source_target_pairs={{0,3},{1,2},{2,1},{3,0},{4,7},{5,6},{6,5},{7,4},{8,11},{9,10},{10,... | collective-permute-start | bytes 3932168 | tf_op jit(solution)/shard_map/cond/branch_0_fun/ppermute | solution.py:422
  175.0 92.4 %all-to-all-start.1 = ((bf16[4,88,5120]{2,1,0:T(8,128)(2,1)}), bf16[4,88,5120]{2,1,0:T(8,128)(2,1)}, u32[]{:S(2)}, u32[]{:S(2)}) async-start(bf16[4,88,5120]{2,1,0:T(8,128)(2,1)} %bitcast.110), calls=%async_computation.1 | async-start | bytes 7208960 | tf_op jit(solution)/shard_map/cond/branch_0_fun/all_to_all | solution.py:441
  179.9 3.4 %collective-permute-start.10 = (bf16[128,5120]{1,0:T(8,128)(2,1)}, bf16[128,5120]{1,0:T(8,128)(2,1)S(1)}, u32[]{:S(2)}, u32[]{:S(2)}) collective-permute-start(bf16[128,5120]{1,0:T(8,128)(2,1)} %get-tuple-element.127), channel_id=1, source_target_pairs={{0,1},{1,0},{2,3},{3,2},{4,5},{5,4},{6,7},{7,6},{8,9},{9,8},{10,11... | collective-permute-start | bytes 3932168 | tf_op jit(solution)/shard_map/cond/branch_0_fun/ppermute | solution.py:422
  180.4 30.7 %collective-permute-start.11 = (bf16[128,5120]{1,0:T(8,128)(2,1)}, bf16[128,5120]{1,0:T(8,128)(2,1)S(1)}, u32[]{:S(2)}, u32[]{:S(2)}) collective-permute-start(bf16[128,5120]{1,0:T(8,128)(2,1)} %get-tuple-element.128), channel_id=1, source_target_pairs={{0,2},{1,3},{2,0},{3,1},{4,6},{5,7},{6,4},{7,5},{8,10},{9,11},{10,... | collective-permute-start | bytes 3932168 | tf_op jit(solution)/shard_map/cond/branch_0_fun/ppermute | solution.py:422
  181.0 59.1 %collective-permute-start.12 = (bf16[128,5120]{1,0:T(8,128)(2,1)}, bf16[128,5120]{1,0:T(8,128)(2,1)S(1)}, u32[]{:S(2)}, u32[]{:S(2)}) collective-permute-start(bf16[128,5120]{1,0:T(8,128)(2,1)} %get-tuple-element.129), channel_id=1, source_target_pairs={{0,3},{1,2},{2,1},{3,0},{4,7},{5,6},{6,5},{7,4},{8,11},{9,10},{10,... | collective-permute-start | bytes 3932168 | tf_op jit(solution)/shard_map/cond/branch_0_fun/ppermute | solution.py:422
  182.2 66.1 %collective-permute-start.7 = (bf16[1280,256]{1,0:T(8,128)(2,1)}, bf16[1280,256]{1,0:T(8,128)(2,1)S(1)}, u32[]{:S(2)}, u32[]{:S(2)}) collective-permute-start(bf16[1280,256]{1,0:T(8,128)(2,1)} %get-tuple-element.123), channel_id=1, source_target_pairs={{0,1},{1,0},{2,3},{3,2},{4,5},{5,4},{6,7},{7,6},{8,9},{9,8},{10,11... | collective-permute-start | bytes 1966088 | tf_op jit(solution)/shard_map/cond/branch_0_fun/ppermute | solution.py:422
  182.3 70.9 %collective-permute-start.8 = (bf16[1280,256]{1,0:T(8,128)(2,1)}, bf16[1280,256]{1,0:T(8,128)(2,1)S(1)}, u32[]{:S(2)}, u32[]{:S(2)}) collective-permute-start(bf16[1280,256]{1,0:T(8,128)(2,1)} %get-tuple-element.124), channel_id=1, source_target_pairs={{0,2},{1,3},{2,0},{3,1},{4,6},{5,7},{6,4},{7,5},{8,10},{9,11},{10,... | collective-permute-start | bytes 1966088 | tf_op jit(solution)/shard_map/cond/branch_0_fun/ppermute | solution.py:422
  183.3 84.0 %collective-permute-start.9 = (bf16[1280,256]{1,0:T(8,128)(2,1)}, bf16[1280,256]{1,0:T(8,128)(2,1)S(1)}, u32[]{:S(2)}, u32[]{:S(2)}) collective-permute-start(bf16[1280,256]{1,0:T(8,128)(2,1)} %get-tuple-element.125), channel_id=1, source_target_pairs={{0,3},{1,2},{2,1},{3,0},{4,7},{5,6},{6,5},{7,4},{8,11},{9,10},{10,... | collective-permute-start | bytes 1966088 | tf_op jit(solution)/shard_map/cond/branch_0_fun/ppermute | solution.py:422
  (24 other events, 289.2 us)
where the time goes:
time: 275 us; the launch traced here: 274 us
  waiting for transfers between devices  169 us (61%)
  Pallas kernels  48.9 us (18%)
  starting transfers between devices  40.4 us (15%)
  other arithmetic  6.76 us (2%)
  local copies, waits for them, and re-layouts  6.03 us (2%)
  between operations  2.87 us (1%)
    ppermute x12, waiting for transfers between devices, near(): lax.ppermute(bufs[s], 'dp', [(d, d ^ s) for d in range(devices)])  87.2 us
    pallas_call x14, Pallas kernels, call(): pl.pallas_call(kernel, grid=(pieces,), in_specs=in_specs + [HERE] * len(a...  48.9 us
    all_to_all x2, waiting for transfers between devices, planes_swap(): lax.all_to_all(x, 'dp', split_axis=0, concat_axis=0, tiled=True, axis_ind...  41.7 us
    all_to_all x1, waiting for transfers between devices, shards(): lax.all_to_all(note, ('groups', 'dp'), split_axis=0, concat_axis=0, tiled...  19.6 us
    all_to_all x2, starting transfers between devices, planes_swap(): lax.all_to_all(x, 'dp', split_axis=0, concat_axis=0, tiled=True, axis_ind...  13.2 us
    ppermute x3, waiting for transfers between devices, across(): lax.ppermute(bufs[s], 'dp', [(d, (d // column ^ s) * column + d % column)...  11 us
    ppermute x12, starting transfers between devices, near(): lax.ppermute(bufs[s], 'dp', [(d, d ^ s) for d in range(devices)])  9.51 us
    ppermute x1, waiting for transfers between devices, run(): weight = (weight_z, lax.ppermute(weight_z, 'groups', [(0, 1), (1, 0)]))  9.32 us
  transfers between devices with their start and end apart: 25, of which 12 were waited for; matrix products, arithmetic and copies ran while one was open for 3% of the time, Pallas kernels for 14%

commit v1 on v0

--- a/solution.py
+++ b/solution.py
@@ -351,45 +351,13 @@
             for s in range(1, PLANES)
         ]
         first.last = [own_share]
-        note = note_step(first, note[None])[0]
         near_share, far_shares = shares[1:2], shares[2:]
         shares = jnp.stack(shares)
         turn = jnp.arange(PLANES, dtype=jnp.int32) ^ plane
         weight_z = shares[0][None]
         for s in range(1, PLANES):
             weight_z = jnp.where((turn == s)[:, None, None], shares[s][None], weight_z)
-    note = jnp.broadcast_to(note[None, None], (parts * devices, 1, tok_rows + 128))
-    first.last = [note]
-    notes = lax.all_to_all(
-        note,
-        ("groups", "dp"),
-        split_axis=0,
-        concat_axis=0,
-        tiled=True,
-    )[:, 0]
-    need_all = jnp.max(notes[:, tok_rows])
-    mine = notes[:, :tok_rows].reshape(parts, PLANES, column, tok_rows)
-    mine = lax.dynamic_index_in_dim(mine, lax.axis_index("groups"), 0, keepdims=False)
-    mine = lax.dynamic_index_in_dim(mine, place, 1, keepdims=False)
-    slots = mine
-    goal = slots // (local * column)
     earlier = jnp.arange(tok_rows)[None, :] < jnp.arange(tok_rows)[:, None]
-    order = jnp.sum(
-        ((goal[:, :, None] == goal[:, None, :]) & earlier[None]).astype(jnp.int32), axis=2
-    )
-    rank = jnp.sum(
-        ((slots[:, :, None] == slots[:, None, :]) & earlier[None]).astype(jnp.int32), axis=2
-    )
-    owner = (slots // local) % column
-    if ring:
-        owner = owner ^ place
-    spot = (
-        owner * (local * segment)
-        + (slots % local) * segment
-        + planes[:, None] * depth
-        + rank
-    )
-    spot = jnp.where(goal == plane, spot, -1)
     own_goal = row_slot // (local * column)
     own_order = jnp.sum(
         ((own_goal[:, None] == own_goal[None, :]) & earlier).astype(jnp.int32), axis=1
@@ -490,6 +458,38 @@
         mates = mates[:column]
         first.last += far_shares
     scaled_z = across(route(first, rows_out, [scaled], [most] * PLANES))
+    if ring:
+        note = note_step(first, note[None])[0]
+    note = jnp.broadcast_to(note[None, None], (parts * devices, 1, tok_rows + 128))
+    notes = lax.all_to_all(
+        note,
+        ("groups", "dp"),
+        split_axis=0,
+        concat_axis=0,
+        tiled=True,
+    )[:, 0]
+    need_all = jnp.max(notes[:, tok_rows])
+    mine = notes[:, :tok_rows].reshape(parts, PLANES, column, tok_rows)
+    mine = lax.dynamic_index_in_dim(mine, lax.axis_index("groups"), 0, keepdims=False)
+    mine = lax.dynamic_index_in_dim(mine, place, 1, keepdims=False)
+    slots = mine
+    goal = slots // (local * column)
+    order = jnp.sum(
+        ((goal[:, :, None] == goal[:, None, :]) & earlier[None]).astype(jnp.int32), axis=2
+    )
+    rank = jnp.sum(
+        ((slots[:, :, None] == slots[:, None, :]) & earlier[None]).astype(jnp.int32), axis=2
+    )
+    owner = (slots // local) % column
+    if ring:
+        owner = owner ^ place
+    spot = (
+        owner * (local * segment)
+        + (slots % local) * segment
+        + planes[:, None] * depth
+        + rank
+    )
+    spot = jnp.where(goal == plane, spot, -1)
     steps = [most * 11 // 16, most * 13 // 16, most]
     total = PLANES * steps[0]
     usual = route(first, outward(steps[0], own_goal)[0], [acts], [total])[0]

time: 275 us -> 270 us (0.982)
  waiting for transfers between devices: 169 us -> 153 us
  starting transfers between devices: 40.4 us -> 50.4 us
    all_to_all x1, waiting for transfers between devices: 19.6 us -> 0.01 us  [shards(): lax.all_to_all(note, ('groups', 'dp'), split_axis=0, concat_axis=0, tiled...]
    ppermute x3, waiting for transfers between devices: 0.01 us -> 8 us  [shards(): lax.ppermute(own_share, 'dp', [(d, (d // column ^ s) * column + d % colum...]
    all_to_all x1, starting transfers between devices: 7.04 us -> 12.3 us  [shards(): lax.all_to_all(note, ('groups', 'dp'), split_axis=0, concat_axis=0, tiled...]
  transfers between devices with their start and end apart: 25 -> 25, of which waited for: 12 -> 13; matrix products, arithmetic and copies ran while one was open for 3% -> 4% of each run, Pallas kernels for 14% -> 14%
where the time goes in v1:
time: 270 us; the launch traced here: 269 us
  waiting for transfers between devices  153 us (57%)
  starting transfers between devices  50.4 us (19%)
  Pallas kernels  48.2 us (18%)
  other arithmetic  8.66 us (3%)
  local copies, waits for them, and re-layouts  5.28 us (2%)
  between operations  2.83 us (1%)
    ppermute x12, waiting for transfers between devices, near(): lax.ppermute(bufs[s], 'dp', [(d, d ^ s) for d in range(devices)])  85.5 us
    pallas_call x14, Pallas kernels, call(): pl.pallas_call(kernel, grid=(pieces,), in_specs=in_specs + [HERE] * len(a...  48.2 us
    all_to_all x2, waiting for transfers between devices, planes_swap(): lax.all_to_all(x, 'dp', split_axis=0, concat_axis=0, tiled=True, axis_ind...  41.6 us
    all_to_all x2, starting transfers between devices, planes_swap(): lax.all_to_all(x, 'dp', split_axis=0, concat_axis=0, tiled=True, axis_ind...  13.2 us
    all_to_all x1, starting transfers between devices, shards(): lax.all_to_all(note, ('groups', 'dp'), split_axis=0, concat_axis=0, tiled...  12.3 us
    ppermute x12, starting transfers between devices, near(): lax.ppermute(bufs[s], 'dp', [(d, d ^ s) for d in range(devices)])  10.5 us
    ppermute x1, waiting for transfers between devices, run(): weight = (weight_z, lax.ppermute(weight_z, 'groups', [(0, 1), (1, 0)]))  9.39 us
    ppermute x3, waiting for transfers between devices, across(): lax.ppermute(bufs[s], 'dp', [(d, (d // column ^ s) * column + d % column)...  8.32 us
  transfers between devices with their start and end apart: 25, of which 13 were waited for; matrix products, arithmetic and copies ran while one was open for 4% of the time, Pallas kernels for 14%

profile of v1, /device:TPU:1, one launch (start us, length us, event | category | flops | bytes accessed | tf_op | source)
XLA Modules:
  0.0 268.5 jit_solution(16587757553831031139)
XLA Ops:
  12.4 5.3 %collective-permute-done.39.refs_3_ = bf16[160,1024]{1,0:T(8,128)(2,1)S(1)} collective-permute-done((bf16[160,1024]{1,0:T(8,128)(2,1)S(1)}, bf16[160,1024]{1,0:T(8,128)(2,1)S(1)}, u32[]{:S(2)}, u32[]{:S(2)}) %collective-permute-start.39) | collective-permute-done | bytes 327712 | tf_op jit(solution)/shard_map/ppermute | solution.py:346
  24.6 2.7 %collective-permute-done.42.refs_4_ = bf16[160,1024]{1,0:T(8,128)(2,1)S(1)} collective-permute-done((bf16[160,1024]{1,0:T(8,128)(2,1)S(1)}, bf16[160,1024]{1,0:T(8,128)(2,1)S(1)}, u32[]{:S(2)}, u32[]{:S(2)}) %collective-permute-start.42) | collective-permute-done | bytes 327712 | tf_op jit(solution)/shard_map/ppermute | solution.py:346
  30.2 12.3 %all-to-all-start.6 = ((s32[32,1,384]{2,1,0:T(1,128)}), s32[32,1,384]{2,1,0:T(1,128)S(1)}, u32[]{:S(2)}, u32[]{:S(2)}) async-start(s32[32,1,384]{2,1,0:T(1,128)} %broadcast_in_dim.177), calls=%async_computation.6 | async-start | bytes 98304 | tf_op jit(solution)/shard_map/all_to_all | solution.py:464
  47.4 2.5 collective-permute-start.47
  49.9 3.4 %shard_map.107 = (bf16[352,5120]{1,0:T(8,128)(2,1)}, s32[8,128]{1,0:T(8,128)S(1)}) custom-call(bf16[352,256]{1,0:T(8,128)(2,1)S(1)} %fusion.17.refs_0_, bf16[256,5120]{1,0:T(8,128)(2,1)S(1)} %copy-done.33, s32[8,128]{1,0:T(8,128)S(1)} %get-tuple-element.252.refs_2_), custom_call_target="tpu_custom_call" | custom-call | tf_op jit(solution)/shard_map/pallas_call | solution.py:110
  57.3 7.6 %collective-permute-done.45.refs_4_ = bf16[128,1024]{1,0:T(8,128)(2,1)S(1)} collective-permute-done((bf16[128,1024]{1,0:T(8,128)(2,1)}, bf16[128,1024]{1,0:T(8,128)(2,1)S(1)}, u32[]{:S(2)}, u32[]{:S(2)}) %collective-permute-start.45) | collective-permute-done | bytes 262176 | tf_op jit(solution)/shard_map/ppermute | solution.py:368
  64.9 2.4 shard_map.108
  67.3 200.2 %conditional.1 = (bf16[256,5120]{1,0:T(8,128)(2,1)}, bf16[2,5120,128]{2,1,0:T(8,128)(2,1)}, bf16[2,128,1024]{2,1,0:T(8,128)(2,1)}) conditional(s32[]{:T(128)} %clamp.11, (s32[256]{0:T(256)S(1)}, s32[256]{0:T(256)S(1)}, s32[4,256]{1,0:T(4,128)S(1)}, s32[4,256]{1,0:T(4,128)S(1)}, bf16[128,1024]{1,0:T(8,128)(2,1)}, ...), branch_computations={%region_11.13_spmd, %region_13.15_spmd, %region_15.17_spmd} | conditional | flops 2099712 | bytes 124301464 | solution.py:526
  67.3 8.4 %all-to-all-start = ((bf16[4,88,5120]{2,1,0:T(8,128)(2,1)}), bf16[4,88,5120]{2,1,0:T(8,128)(2,1)}, u32[]{:S(2)}, u32[]{:S(2)}) async-start(bf16[4,88,5120]{2,1,0:T(8,128)(2,1)} %bitcast.109), calls=%async_computation | async-start | bytes 7208960 | tf_op jit(solution)/shard_map/cond/branch_0_fun/all_to_all | solution.py:409
  80.3 5.1 %collective-permute-done.1 = bf16[128,1024]{1,0:T(8,128)(2,1)S(1)} collective-permute-done((bf16[128,1024]{1,0:T(8,128)(2,1)S(1)}, bf16[128,1024]{1,0:T(8,128)(2,1)S(1)}, u32[]{:S(2)}, u32[]{:S(2)}) %collective-permute-start.1) | collective-permute-done | bytes 262176 | tf_op jit(solution)/shard_map/cond/branch_0_fun/ppermute | solution.py:390
  85.4 6.1 %collective-permute-done.2 = bf16[128,1024]{1,0:T(8,128)(2,1)S(1)} collective-permute-done((bf16[128,1024]{1,0:T(8,128)(2,1)}, bf16[128,1024]{1,0:T(8,128)(2,1)S(1)}, u32[]{:S(2)}, u32[]{:S(2)}) %collective-permute-start.2) | collective-permute-done | bytes 262176 | tf_op jit(solution)/shard_map/cond/branch_0_fun/ppermute | solution.py:390
  93.8 3.8 %branch_0_fun.9 = (bf16[2,64,5120]{2,1,0:T(8,128)(2,1)}, bf16[2,64,5120]{2,1,0:T(8,128)(2,1)}, bf16[2,64,5120]{2,1,0:T(8,128)(2,1)}, bf16[2,64,5120]{2,1,0:T(8,128)(2,1)}, s32[8,128]{1,0:T(8,128)S(1)}) custom-call(bf16[2,256,128]{2,1,0:T(8,128)(2,1)S(1)} %get-tuple-element.105.refs_0_, bf16[2,5120,128]{2,1,0:T(8,128)(2,1)S(1)} %copy-done.32, ...), custom_call_target="tpu_custom_call" | custom-call | tf_op jit(solution)/shard_map/cond/branch_0_fun/pallas_call | solution.py:110
  100.3 9.4 %collective-permute-done.6.refs_1_ = bf16[4,160,1024]{2,1,0:T(8,128)(2,1)} collective-permute-done((bf16[4,160,1024]{2,1,0:T(8,128)(2,1)}, bf16[4,160,1024]{2,1,0:T(8,128)(2,1)}, u32[]{:S(2)}, u32[]{:S(2)}) %collective-permute-start.6) | collective-permute-done | bytes 1310752 | tf_op jit(solution)/shard_map/cond/branch_0_fun/ppermute | solution.py:504
  109.7 6.4 %branch_0_fun.10 = (bf16[1280,256]{1,0:T(8,128)(2,1)}, bf16[1280,256]{1,0:T(8,128)(2,1)}, bf16[1280,256]{1,0:T(8,128)(2,1)}, bf16[1280,256]{1,0:T(8,128)(2,1)}, s32[8,128]{1,0:T(8,128)S(1)}) custom-call(bf16[4,160,1024]{2,1,0:T(8,128)(2,1)} %get-tuple-element.113.refs_0_, bf16[4,160,1024]{2,1,0:T(8,128)(2,1)} %collective-permute-done.6.refs_1_, ...), custom_call_target="tpu_custom_call" | custom-call | tf_op jit(solution)/shard_map/cond/branch_0_fun/pallas_call | solution.py:110
  116.1 41.5 %all-to-all-done = bf16[4,88,5120]{2,1,0:T(8,128)(2,1)} async-done(((bf16[4,88,5120]{2,1,0:T(8,128)(2,1)}), bf16[4,88,5120]{2,1,0:T(8,128)(2,1)}, u32[]{:S(2)}, u32[]{:S(2)}) %all-to-all-start) | async-done | bytes 3604512 | tf_op jit(solution)/shard_map/cond/branch_0_fun/all_to_all | solution.py:409
  157.7 6.5 %branch_0_fun.11 = (bf16[128,5120]{1,0:T(8,128)(2,1)}, bf16[128,5120]{1,0:T(8,128)(2,1)}, bf16[128,5120]{1,0:T(8,128)(2,1)}, bf16[128,5120]{1,0:T(8,128)(2,1)}, s32[8,128]{1,0:T(8,128)S(1)}) custom-call(bf16[512,352]{1,0:T(8,128)(2,1)S(1)} %fusion.refs_0_, bf16[352,5120]{1,0:T(8,128)(2,1)} %bitcast.9.refs_1_, s32[8,128]{1,0:T(8,128)S(1)} %get-tuple-element.119.refs_2_), custom_call_target="tpu_custom_call" | custom-call | tf_op jit(solution)/shard_map/cond/branch_0_fun/pallas_call | solution.py:110
  164.2 5.3 %branch_0_fun.12 = (bf16[352,5120]{1,0:T(8,128)(2,1)}, s32[8,128]{1,0:T(8,128)S(1)}) custom-call(bf16[352,512]{1,0:T(8,128)(2,1)S(1)} %fusion.1.refs_0_, bf16[128,5120]{1,0:T(8,128)(2,1)S(1)} %bitcast.80, bf16[128,5120]{1,0:T(8,128)(2,1)S(1)} %collective-permute-done.3.refs_2_, bf16[128,5120]{1,0:T(8,128)(2,1)S(1)} %collective-permute-done.4.refs_3_, ...), custom_call_target="tpu_custom_call" | custom-call | tf_op jit(solution)/shard_map/cond/branch_0_fun/pallas_call | solution.py:110
  169.6 4.9 %all-to-all-start.1 = ((bf16[4,88,5120]{2,1,0:T(8,128)(2,1)}), bf16[4,88,5120]{2,1,0:T(8,128)(2,1)}, u32[]{:S(2)}, u32[]{:S(2)}) async-start(bf16[4,88,5120]{2,1,0:T(8,128)(2,1)} %bitcast.110), calls=%async_computation.1 | async-start | bytes 7208960 | tf_op jit(solution)/shard_map/cond/branch_0_fun/all_to_all | solution.py:409
  179.4 26.2 %collective-permute-done.11 = bf16[128,5120]{1,0:T(8,128)(2,1)S(1)} collective-permute-done((bf16[128,5120]{1,0:T(8,128)(2,1)}, bf16[128,5120]{1,0:T(8,128)(2,1)S(1)}, u32[]{:S(2)}, u32[]{:S(2)}) %collective-permute-start.11) | collective-permute-done | bytes 1310752 | tf_op jit(solution)/shard_map/cond/branch_0_fun/ppermute | solution.py:390
  205.6 29.0 %collective-permute-done.12 = bf16[128,5120]{1,0:T(8,128)(2,1)S(1)} collective-permute-done((bf16[128,5120]{1,0:T(8,128)(2,1)}, bf16[128,5120]{1,0:T(8,128)(2,1)S(1)}, u32[]{:S(2)}, u32[]{:S(2)}) %collective-permute-start.12) | collective-permute-done | bytes 1310752 | tf_op jit(solution)/shard_map/cond/branch_0_fun/ppermute | solution.py:390
  235.6 6.1 %branch_0_fun.13 = (f32[2,256,128]{2,1,0:T(8,128)S(1)}, bf16[2,5120,128]{2,1,0:T(8,128)(2,1)}, s32[8,128]{1,0:T(8,128)S(1)}) custom-call(bf16[2,256,128]{2,1,0:T(8,128)(2,1)S(1)} %copy-done.30, bf16[2,5120,128]{2,1,0:T(8,128)(2,1)} %get-tuple-element.106.refs_1_, bf16[2,64,5120]{2,1,0:T(8,128)(2,1)S(1)} %bitcast.66, bf16[2,64,5120]{2,1,0:T(8,128)(2,1)S(1)} %bitcast.69, ...), custom_call_target="tpu_custom_call" | custom-call | tf_op jit(solution)/shard_map/cond/branch_0_fun/pallas_call | solution.py:110
  242.8 5.0 %collective-permute-done.8.refs_4_ = bf16[1280,256]{1,0:T(8,128)(2,1)S(1)} collective-permute-done((bf16[1280,256]{1,0:T(8,128)(2,1)}, bf16[1280,256]{1,0:T(8,128)(2,1)S(1)}, u32[]{:S(2)}, u32[]{:S(2)}) %collective-permute-start.8) | collective-permute-done | bytes 655392 | tf_op jit(solution)/shard_map/cond/branch_0_fun/ppermute | solution.py:390
  247.8 14.1 %collective-permute-done.9.refs_5_ = bf16[1280,256]{1,0:T(8,128)(2,1)S(1)} collective-permute-done((bf16[1280,256]{1,0:T(8,128)(2,1)}, bf16[1280,256]{1,0:T(8,128)(2,1)S(1)}, u32[]{:S(2)}, u32[]{:S(2)}) %collective-permute-start.9) | collective-permute-done | bytes 655392 | tf_op jit(solution)/shard_map/cond/branch_0_fun/ppermute | solution.py:390
  261.9 5.5 %branch_0_fun.15 = (bf16[256,5120]{1,0:T(8,128)(2,1)}, s32[8,128]{1,0:T(8,128)}) custom-call(bf16[256,352]{1,0:T(8,128)(2,1)S(1)} %fusion.2.refs_0_, bf16[352,5120]{1,0:T(8,128)(2,1)} %bitcast.11.refs_1_, bf16[1280,256]{1,0:T(8,128)(2,1)S(1)} %copy-done.28, bf16[1280,256]{1,0:T(8,128)(2,1)S(1)} %collective-permute-done.7.refs_3_, ...), custom_call_target="tpu_custom_call" | custom-call | tf_op jit(solution)/shard_map/cond/branch_0_fun/pallas_call | solution.py:110
  (135 shorter events, 46.2 us)
Async XLA Ops:
  1.8 15.9 %collective-permute-start.39 = (bf16[160,1024]{1,0:T(8,128)(2,1)S(1)}, bf16[160,1024]{1,0:T(8,128)(2,1)S(1)}, u32[]{:S(2)}, u32[]{:S(2)}) collective-permute-start(bf16[160,1024]{1,0:T(8,128)(2,1)S(1)} %constant_dynamic-slice_fusion.1.refs_2_), channel_id=1, source_target_pairs={{0,4},{1,5},{2,6},{3,7},{4,0},{5,1},{6,2},{7,3},{8,12},{9,13},{10,... | collective-permute-start | bytes 983048 | tf_op jit(solution)/shard_map/ppermute | solution.py:346
  3.9 20.7 %collective-permute-start.41 = (bf16[160,1024]{1,0:T(8,128)(2,1)S(1)}, bf16[160,1024]{1,0:T(8,128)(2,1)S(1)}, u32[]{:S(2)}, u32[]{:S(2)}) collective-permute-start(bf16[160,1024]{1,0:T(8,128)(2,1)S(1)} %constant_dynamic-slice_fusion.1.refs_2_), channel_id=1, source_target_pairs={{0,8},{1,9},{2,10},{3,11},{4,12},{5,13},{6,14},{7,15},{8,0},{9,1},... | collective-permute-start | bytes 983048 | tf_op jit(solution)/shard_map/ppermute | solution.py:346
  6.3 21.1 %collective-permute-start.42 = (bf16[160,1024]{1,0:T(8,128)(2,1)S(1)}, bf16[160,1024]{1,0:T(8,128)(2,1)S(1)}, u32[]{:S(2)}, u32[]{:S(2)}) collective-permute-start(bf16[160,1024]{1,0:T(8,128)(2,1)S(1)} %constant_dynamic-slice_fusion.1.refs_2_), channel_id=1, source_target_pairs={{0,12},{1,13},{2,14},{3,15},{4,8},{5,9},{6,10},{7,11},{8,4},{9,5},... | collective-permute-start | bytes 983048 | tf_op jit(solution)/shard_map/ppermute | solution.py:346
  21.1 46.2 %collective-permute-start.46 = (bf16[256,1024]{1,0:T(8,128)(2,1)}, bf16[256,1024]{1,0:T(8,128)(2,1)}, u32[]{:S(2)}, u32[]{:S(2)}) collective-permute-start(bf16[256,1024]{1,0:T(8,128)(2,1)} %get-tuple-element.244), channel_id=1, source_target_pairs={{0,2},{1,3},{2,0},{3,1},{4,6},{5,7},{6,4},{7,5},{8,10},{9,11},{10,... | collective-permute-start | bytes 1572872 | tf_op jit(solution)/shard_map/ppermute | solution.py:450
  30.2 23.1 %all-to-all-start.6 = ((s32[32,1,384]{2,1,0:T(1,128)}), s32[32,1,384]{2,1,0:T(1,128)S(1)}, u32[]{:S(2)}, u32[]{:S(2)}) async-start(s32[32,1,384]{2,1,0:T(1,128)} %broadcast_in_dim.177), calls=%async_computation.6 | async-start | bytes 98304 | tf_op jit(solution)/shard_map/all_to_all | solution.py:464
  43.9 13.5 %collective-permute-start.43 = (bf16[128,1024]{1,0:T(8,128)(2,1)}, bf16[128,1024]{1,0:T(8,128)(2,1)S(1)}, u32[]{:S(2)}, u32[]{:S(2)}) collective-permute-start(bf16[128,1024]{1,0:T(8,128)(2,1)} %get-tuple-element.249), channel_id=1, source_target_pairs={{0,4},{1,5},{2,6},{3,7},{4,0},{5,1},{6,2},{7,3},{8,12},{9,13},{10,... | collective-permute-start | bytes 786440 | tf_op jit(solution)/shard_map/ppermute | solution.py:368
  45.3 12.1 %collective-permute-start.44 = (bf16[128,1024]{1,0:T(8,128)(2,1)}, bf16[128,1024]{1,0:T(8,128)(2,1)S(1)}, u32[]{:S(2)}, u32[]{:S(2)}) collective-permute-start(bf16[128,1024]{1,0:T(8,128)(2,1)} %get-tuple-element.250), channel_id=1, source_target_pairs={{0,8},{1,9},{2,10},{3,11},{4,12},{5,13},{6,14},{7,15},{8,0},{9,1},... | collective-permute-start | bytes 786440 | tf_op jit(solution)/shard_map/ppermute | solution.py:368
  47.4 17.5 %collective-permute-start.45 = (bf16[128,1024]{1,0:T(8,128)(2,1)}, bf16[128,1024]{1,0:T(8,128)(2,1)S(1)}, u32[]{:S(2)}, u32[]{:S(2)}) collective-permute-start(bf16[128,1024]{1,0:T(8,128)(2,1)} %get-tuple-element.251), channel_id=1, source_target_pairs={{0,12},{1,13},{2,14},{3,15},{4,8},{5,9},{6,10},{7,11},{8,4},{9,5},... | collective-permute-start | bytes 786440 | tf_op jit(solution)/shard_map/ppermute | solution.py:368
  47.4 19.8 %collective-permute-start.47 = (bf16[256,1024]{1,0:T(8,128)(2,1)S(1)}, bf16[256,1024]{1,0:T(8,128)(2,1)}, u32[]{:S(2)}, u32[]{:S(2)}) collective-permute-start(bf16[256,1024]{1,0:T(8,128)(2,1)S(1)} %copy-done.48), channel_id=1, source_target_pairs={{0,3},{1,2},{2,1},{3,0},{4,7},{5,6},{6,5},{7,4},{8,11},{9,10},{10,... | collective-permute-start | bytes 1572872 | tf_op jit(solution)/shard_map/ppermute | solution.py:455
  67.3 90.3 %all-to-all-start = ((bf16[4,88,5120]{2,1,0:T(8,128)(2,1)}), bf16[4,88,5120]{2,1,0:T(8,128)(2,1)}, u32[]{:S(2)}, u32[]{:S(2)}) async-start(bf16[4,88,5120]{2,1,0:T(8,128)(2,1)} %bitcast.109), calls=%async_computation | async-start | bytes 7208960 | tf_op jit(solution)/shard_map/cond/branch_0_fun/all_to_all | solution.py:409
  75.7 4.6 %collective-permute-start = (bf16[128,1024]{1,0:T(8,128)(2,1)S(1)}, bf16[128,1024]{1,0:T(8,128)(2,1)S(1)}, u32[]{:S(2)}, u32[]{:S(2)}) collective-permute-start(bf16[128,1024]{1,0:T(8,128)(2,1)S(1)} %copy-done.49), channel_id=1, source_target_pairs={{0,1},{1,0},{2,3},{3,2},{4,5},{5,4},{6,7},{7,6},{8,9},{9,8},{10,11... | collective-permute-start | bytes 786440 | tf_op jit(solution)/shard_map/cond/branch_0_fun/ppermute | solution.py:390
  77.4 8.0 %collective-permute-start.1 = (bf16[128,1024]{1,0:T(8,128)(2,1)S(1)}, bf16[128,1024]{1,0:T(8,128)(2,1)S(1)}, u32[]{:S(2)}, u32[]{:S(2)}) collective-permute-start(bf16[128,1024]{1,0:T(8,128)(2,1)S(1)} %copy-done.52), channel_id=1, source_target_pairs={{0,2},{1,3},{2,0},{3,1},{4,6},{5,7},{6,4},{7,5},{8,10},{9,11},{10,... | collective-permute-start | bytes 786440 | tf_op jit(solution)/shard_map/cond/branch_0_fun/ppermute | solution.py:390
  78.6 12.9 %collective-permute-start.2 = (bf16[128,1024]{1,0:T(8,128)(2,1)}, bf16[128,1024]{1,0:T(8,128)(2,1)S(1)}, u32[]{:S(2)}, u32[]{:S(2)}) collective-permute-start(bf16[128,1024]{1,0:T(8,128)(2,1)} %get-tuple-element.104), channel_id=1, source_target_pairs={{0,3},{1,2},{2,1},{3,0},{4,7},{5,6},{6,5},{7,4},{8,11},{9,10},{10,... | collective-permute-start | bytes 786440 | tf_op jit(solution)/shard_map/cond/branch_0_fun/ppermute | solution.py:390
  79.1 30.5 %collective-permute-start.6 = (bf16[4,160,1024]{2,1,0:T(8,128)(2,1)}, bf16[4,160,1024]{2,1,0:T(8,128)(2,1)}, u32[]{:S(2)}, u32[]{:S(2)}) collective-permute-start(bf16[4,160,1024]{2,1,0:T(8,128)(2,1)} %get-tuple-element.113.refs_0_), channel_id=1, source_target_pairs={{0,16},{16,0},{1,17},{17,1},{2,18},{18,2},{3,19},{19,3},{4,20},{20... | collective-permute-start | bytes 3932168 | tf_op jit(solution)/shard_map/cond/branch_0_fun/ppermute | solution.py:504
  97.6 66.6 %collective-permute-start.3 = (bf16[128,5120]{1,0:T(8,128)(2,1)}, bf16[128,5120]{1,0:T(8,128)(2,1)S(1)}, u32[]{:S(2)}, u32[]{:S(2)}) collective-permute-start(bf16[128,5120]{1,0:T(8,128)(2,1)} %bitcast.123), channel_id=1, source_target_pairs={{0,1},{1,0},{2,3},{3,2},{4,5},{5,4},{6,7},{7,6},{8,9},{9,8},{10,11... | collective-permute-start | bytes 3932168 | tf_op jit(solution)/shard_map/cond/branch_0_fun/ppermute | solution.py:390
  97.6 66.5 %collective-permute-start.4 = (bf16[128,5120]{1,0:T(8,128)(2,1)}, bf16[128,5120]{1,0:T(8,128)(2,1)S(1)}, u32[]{:S(2)}, u32[]{:S(2)}) collective-permute-start(bf16[128,5120]{1,0:T(8,128)(2,1)} %bitcast.120), channel_id=1, source_target_pairs={{0,2},{1,3},{2,0},{3,1},{4,6},{5,7},{6,4},{7,5},{8,10},{9,11},{10,... | collective-permute-start | bytes 3932168 | tf_op jit(solution)/shard_map/cond/branch_0_fun/ppermute | solution.py:390
  98.9 65.3 %collective-permute-start.5 = (bf16[128,5120]{1,0:T(8,128)(2,1)}, bf16[128,5120]{1,0:T(8,128)(2,1)}, u32[]{:S(2)}, u32[]{:S(2)}) collective-permute-start(bf16[128,5120]{1,0:T(8,128)(2,1)} %bitcast.117), channel_id=1, source_target_pairs={{0,3},{1,2},{2,1},{3,0},{4,7},{5,6},{6,5},{7,4},{8,11},{9,10},{10,... | collective-permute-start | bytes 3932168 | tf_op jit(solution)/shard_map/cond/branch_0_fun/ppermute | solution.py:390
  169.6 92.3 %all-to-all-start.1 = ((bf16[4,88,5120]{2,1,0:T(8,128)(2,1)}), bf16[4,88,5120]{2,1,0:T(8,128)(2,1)}, u32[]{:S(2)}, u32[]{:S(2)}) async-start(bf16[4,88,5120]{2,1,0:T(8,128)(2,1)} %bitcast.110), calls=%async_computation.1 | async-start | bytes 7208960 | tf_op jit(solution)/shard_map/cond/branch_0_fun/all_to_all | solution.py:409
  174.4 3.6 %collective-permute-start.10 = (bf16[128,5120]{1,0:T(8,128)(2,1)}, bf16[128,5120]{1,0:T(8,128)(2,1)S(1)}, u32[]{:S(2)}, u32[]{:S(2)}) collective-permute-start(bf16[128,5120]{1,0:T(8,128)(2,1)} %get-tuple-element.127), channel_id=1, source_target_pairs={{0,1},{1,0},{2,3},{3,2},{4,5},{5,4},{6,7},{7,6},{8,9},{9,8},{10,11... | collective-permute-start | bytes 3932168 | tf_op jit(solution)/shard_map/cond/branch_0_fun/ppermute | solution.py:390
  175.0 30.7 %collective-permute-start.11 = (bf16[128,5120]{1,0:T(8,128)(2,1)}, bf16[128,5120]{1,0:T(8,128)(2,1)S(1)}, u32[]{:S(2)}, u32[]{:S(2)}) collective-permute-start(bf16[128,5120]{1,0:T(8,128)(2,1)} %get-tuple-element.128), channel_id=1, source_target_pairs={{0,2},{1,3},{2,0},{3,1},{4,6},{5,7},{6,4},{7,5},{8,10},{9,11},{10,... | collective-permute-start | bytes 3932168 | tf_op jit(solution)/shard_map/cond/branch_0_fun/ppermute | solution.py:390
  176.2 58.5 %collective-permute-start.12 = (bf16[128,5120]{1,0:T(8,128)(2,1)}, bf16[128,5120]{1,0:T(8,128)(2,1)S(1)}, u32[]{:S(2)}, u32[]{:S(2)}) collective-permute-start(bf16[128,5120]{1,0:T(8,128)(2,1)} %get-tuple-element.129), channel_id=1, source_target_pairs={{0,3},{1,2},{2,1},{3,0},{4,7},{5,6},{6,5},{7,4},{8,11},{9,10},{10,... | collective-permute-start | bytes 3932168 | tf_op jit(solution)/shard_map/cond/branch_0_fun/ppermute | solution.py:390
  176.7 66.1 %collective-permute-start.7 = (bf16[1280,256]{1,0:T(8,128)(2,1)}, bf16[1280,256]{1,0:T(8,128)(2,1)S(1)}, u32[]{:S(2)}, u32[]{:S(2)}) collective-permute-start(bf16[1280,256]{1,0:T(8,128)(2,1)} %get-tuple-element.123), channel_id=1, source_target_pairs={{0,1},{1,0},{2,3},{3,2},{4,5},{5,4},{6,7},{7,6},{8,9},{9,8},{10,11... | collective-permute-start | bytes 1966088 | tf_op jit(solution)/shard_map/cond/branch_0_fun/ppermute | solution.py:390
  176.9 70.9 %collective-permute-start.8 = (bf16[1280,256]{1,0:T(8,128)(2,1)}, bf16[1280,256]{1,0:T(8,128)(2,1)S(1)}, u32[]{:S(2)}, u32[]{:S(2)}) collective-permute-start(bf16[1280,256]{1,0:T(8,128)(2,1)} %get-tuple-element.124), channel_id=1, source_target_pairs={{0,2},{1,3},{2,0},{3,1},{4,6},{5,7},{6,4},{7,5},{8,10},{9,11},{10,... | collective-permute-start | bytes 1966088 | tf_op jit(solution)/shard_map/cond/branch_0_fun/ppermute | solution.py:390
  178.0 83.8 %collective-permute-start.9 = (bf16[1280,256]{1,0:T(8,128)(2,1)}, bf16[1280,256]{1,0:T(8,128)(2,1)S(1)}, u32[]{:S(2)}, u32[]{:S(2)}) collective-permute-start(bf16[1280,256]{1,0:T(8,128)(2,1)} %get-tuple-element.125), channel_id=1, source_target_pairs={{0,3},{1,2},{2,1},{3,0},{4,7},{5,6},{6,5},{7,4},{8,11},{9,10},{10,... | collective-permute-start | bytes 1966088 | tf_op jit(solution)/shard_map/cond/branch_0_fun/ppermute | solution.py:390
  (24 other events, 280.3 us)
